TPU v7x, 256 devices: a whole 4x4x8 slice. The times are simulated.
256 devices in a mesh: rep: 2 (over core), section: 4 (over y), exp: 32 (over z, x).
Axes of the slice: x: 4, y: 4, z: 8, core: 2. Of those that a mesh axis runs over, the one named last changes fastest.
Arguments:
- row_codes: bfloat16 [4, 4096, 2048], P('section', ('rep', 'exp')), may hold values from -448 to 448
- block_exponents: int32 [4, 4096, 16], P('section', ('rep', 'exp')), may hold values from -10 to -6
- routes: int32 [4, 4096, 8], P('section', ('rep', 'exp')), may hold values from 0 to 63, all different within a row; in each aligned block of 64 rows (0 to 63, 64 to 127, ..., all dimensions but the last counted through in order) at most 12 rows name the same one
- route_weight: float32 [4, 4096, 8], P('section', ('rep', 'exp')), may hold values from 0.02 to 0.3
- out_grad: bfloat16 [4, 4096, 2048], P('section', ('rep', 'exp')), may hold values from -6 to 6
- gate_weight: bfloat16 [4, 64, 384, 2048], P('section', 'exp', 'rep'), may hold values from -0.125 to 0.125
- up_weight: bfloat16 [4, 64, 384, 2048], P('section', 'exp', 'rep'), may hold values from -0.125 to 0.125
- down_weight: bfloat16 [4, 64, 384, 2048], P('section', 'exp', 'rep'), may hold values from -0.3125 to 0.3125
Outputs:
- next_rows: bfloat16 [4, 4096, 2048], P('section', ('rep', 'exp'))
- prev_grads: bfloat16 [4, 4096, 2048], P('section', ('rep', 'exp'))
- gate_weight_grad: bfloat16 [4, 64, 384, 2048], P('section', 'exp', 'rep')
- up_weight_grad: bfloat16 [4, 64, 384, 2048], P('section', 'exp', 'rep')
- down_weight_grad: bfloat16 [4, 64, 384, 2048], P('section', 'exp', 'rep')
Inputs may be any that keep to these rules, and one draw needn't show every extreme that they name: `routes`: the 8 experts of a token differ. In the 64 rows of one device of a layer no expert is named by more than 12 rows, a bound that some of them reach.
All inputs are finite; a program needn't handle non-finite values.
Results may differ from a plain program's by a relative error of at most 0.0065.
Values may be sent and summed in bfloat16 or wider, within the bound.
A program may use at most 128 MiB of HBM per device.

v0:
```python
import functools

import jax
import jax.numpy as jnp
from jax import lax
from jax.experimental import pallas as pl
from jax.experimental.pallas import tpu as pltpu
from jax.sharding import PartitionSpec as P

MESH = pl.DeviceIdType.MESH
NX = 4
NZ = 8
CAP = 12
ORDER = (0, 1, 7, 2, 6, 3, 5, 4)
PLACE = tuple(ORDER.index(slot) for slot in range(NZ))
TILE = 512
F32 = jnp.float32
BF16 = jnp.bfloat16


def dot_nn(a, b):
    return lax.dot_general(a, b, (((1,), (0,)), ((), ())), preferred_element_type=F32)


def dot_nt(a, b):
    return lax.dot_general(a, b, (((1,), (1,)), ((), ())), preferred_element_type=F32)


def kernel(
    codes_ref, exps_ref, routes_ref, rweight_ref, grad_ref, gate_ref, up_ref, down_ref,
    next_ref, prev_ref, gate_out, up_out, down_out,
    zrows, sendrows, arrived, weights, results, returned, reduced, partial, wrecv, final,
    act, hidden, hidden_t, grads, grads_t, meta_src, meta, pick, pick_t, pick_hi, pick_lo, slot_w,
    ring_s, ring_r, meta_s, meta_r, wt_l, wt_s, wt_r, disp_s, disp_r, ret_s, ret_r,
    red_s, red_r, hop_s, hop_r, wg_s, wg_r, out_l,
):
    tokens, width = codes_ref.shape
    unit = sendrows.shape[1]
    half_rows = tokens // 2
    rows = NX * 2 * unit
    half = gate_ref.shape[1]
    full = 2 * half
    tiles = width // TILE
    rep, sec, ex = lax.axis_index("rep"), lax.axis_index("section"), lax.axis_index("exp")
    sections = lax.axis_size("section")
    z, x = lax.div(ex, NX), lax.rem(ex, NX)

    def at_z(k):
        return (rep, sec, lax.rem(z + k, NZ) * NX + x)

    def at_x(k):
        return (rep, sec, z * NX + lax.rem(x + k, NX))

    other_core = (1 - rep, sec, ex)
    sec_next = (rep, lax.rem(sec + 1, sections), ex)
    sec_prev = (rep, lax.rem(sec + sections - 1, sections), ex)

    def remote(src, dst, send, recv, device):
        copy = pltpu.make_async_remote_copy(
            src_ref=src, dst_ref=dst, send_sem=send, recv_sem=recv,
            device_id=device, device_id_type=MESH)
        return copy

    def cols_of(n, size=TILE):
        return pl.ds(pl.multiple_of(n * size, size), size)

    weight_refs = (gate_ref, up_ref, down_ref)
    own_copies = []
    for m in range(3):
        copy = pltpu.make_async_copy(
            weight_refs[m], weights.at[:, pl.ds(m * full, half)], wt_l.at[m])
        copy.start()
        own_copies.append(copy)
    partners = [at_z(k) for k in range(1, NZ)] + [at_x(k) for k in range(1, NX)]
    partners += [other_core, sec_next, sec_prev]
    barrier = pltpu.get_barrier_semaphore()
    for device in partners:
        pl.semaphore_signal(barrier, inc=1, device_id=device, device_id_type=MESH)

    for b in range(width // 128):
        cols = pl.ds(b * 128, 128)
        scale = jnp.exp2(exps_ref[:, b:b + 1].astype(F32))
        zrows[0, 0, :, cols] = (codes_ref[:, cols].astype(F32) * scale).astype(BF16)
    zrows[1, 0] = grad_ref[...]
    pl.semaphore_wait(barrier, len(partners))

    def ring_copy(t, way, step):
        slot = step - 1 if way == 0 else (NZ - step + 1) % NZ
        there = step if way == 0 else NZ - step
        src, dst = zrows.at[t, PLACE[slot]], zrows.at[t, PLACE[there]]
        if step == NZ // 2:
            part = pl.ds(way * half_rows, half_rows)
            src, dst = src.at[part], dst.at[part]
        return remote(src, dst, ring_s.at[t, way, step - 1], ring_r.at[t, way, step - 1],
                      at_z(1 if way == 0 else NZ - 1))

    ring = [[[ring_copy(t, way, step) for step in range(1, 5)] for way in range(2)] for t in range(2)]

    def ring_start(t, step):
        for way in range(2):
            ring[t][way][step - 1].start()

    def ring_wait(t, step):
        for way in range(2):
            ring[t][way][step - 1].wait_recv()

    ring_start(0, 1)

    experts = meta_src.shape[0] * 8
    lanes = 4 * tokens
    expert_id = lax.broadcasted_iota(jnp.int32, (experts, lanes), 0)
    hit = jnp.zeros((experts, lanes), F32)
    weight = jnp.zeros((experts, lanes), F32)
    for k in range(routes_ref.shape[0]):
        same = routes_ref[k:k + 1, :] == expert_id
        hit = jnp.where(same, 1.0, hit)
        weight = jnp.where(same, rweight_ref[k:k + 1, :], weight)
    earlier = lax.broadcasted_iota(jnp.int32, (128, lanes), 0)
    later = lax.rem(lax.broadcasted_iota(jnp.int32, (128, lanes), 1), tokens)
    before = jnp.where((earlier < later) & (earlier < tokens), 1.0, 0.0).astype(BF16)
    count = dot_nn(hit[:, :128].astype(BF16), before)
    slots = jnp.where(hit > 0.5, count, -1.0)
    for g in range(NZ):
        meta_src[g, 0] = slots[g * 8:(g + 1) * 8]
        meta_src[g, 1] = weight[g * 8:(g + 1) * 8]
    meta_copies = []
    for k in range(1, NZ):
        copy = remote(meta_src.at[lax.rem(z + k, NZ)], meta.at[k], meta_s.at[k], meta_r.at[k], at_z(k))
        copy.start()
        meta_copies.append(copy)
    meta_own = pltpu.make_async_copy(meta_src.at[z], meta.at[0], meta_s.at[0])
    meta_own.start()

    weight_copies = []
    for m in range(3):
        copy = remote(weight_refs[m], weights.at[:, pl.ds(m * full + half, half)],
                      wt_s.at[m], wt_r.at[m], other_core)
        copy.start()
        weight_copies.append(copy)

    meta_own.wait()
    for copy in meta_copies:
        copy.wait_recv()

    lane_of = lax.broadcasted_iota(jnp.int32, (unit, lanes), 1)
    row_of = lax.broadcasted_iota(jnp.int32, (unit, lanes), 0)
    target = jnp.where(lax.div(lane_of, tokens) == lax.div(row_of, CAP), lax.rem(row_of, CAP), -5).astype(F32)
    source_of = lax.div(lax.broadcasted_iota(jnp.int32, (8, lanes), 1), tokens)
    for c in range(2):
        slot_cat = jnp.zeros((8, lanes), F32)
        weight_cat = jnp.zeros((8, lanes), F32)
        for q in range(4):
            slot_cat = jnp.where(source_of == q, meta[ORDER[4 * c + q], 0], slot_cat)
            weight_cat = jnp.where(source_of == q, meta[ORDER[4 * c + q], 1], weight_cat)
        for e in range(8):
            same = slot_cat[e:e + 1, :] == target
            weighted = jnp.where(same, weight_cat[e:e + 1, :], 0.0)
            span = pl.ds(e * unit, unit)
            pick[c, span, :] = jnp.where(same, 1.0, 0.0).astype(BF16)
            slot_w[c, span, :] = jnp.broadcast_to(jnp.sum(weighted, axis=1, keepdims=True), (unit, 128))
            act[0, span, pl.ds(0, lanes)] = weighted
            act[1, span, pl.ds(0, lanes)] = jnp.where(same, 1.0, 0.0)
        weighted_t = act[0, :, pl.ds(0, lanes)].T
        high = weighted_t.astype(BF16)
        pick_hi[c] = high
        pick_lo[c] = (weighted_t - high.astype(F32)).astype(BF16)
        pick_t[c] = act[1, :, pl.ds(0, lanes)].T.astype(BF16)

    disp = {}

    def dispatch(t, c):
        base = (t * 2 + c) * NX * 2

        def tile(n, carry):
            cols = cols_of(n)
            taken = zrows[t, pl.ds(4 * c, 4), :, cols].reshape(4 * tokens, TILE)
            chosen = dot_nn(pick[c], taken)
            if t == 1:
                chosen = chosen * slot_w[c][:, :1]
            sendrows[pl.ds(base, 2 * NX), :, cols] = chosen.astype(BF16).reshape(2 * NX, unit, TILE)
            return carry

        lax.fori_loop(0, tiles, tile, 0)
        for d in (2, 1, 3):
            copy = remote(sendrows.at[pl.ds(base + 2 * lax.rem(x + d, NX), 2)], arrived.at[t, :, c, d],
                          disp_s.at[t, c, d], disp_r.at[t, c, d], at_x(d))
            copy.start()
            disp[t, c, d] = copy
        copy = pltpu.make_async_copy(
            sendrows.at[pl.ds(base + 2 * x, 2)], arrived.at[t, :, c, 0], disp_s.at[t, c, 0])
        copy.start()
        disp[t, c, 0] = copy

    def dispatched(t):
        for c in range(2):
            disp[t, c, 0].wait()
            for d in range(1, NX):
                disp[t, c, d].wait_recv()

    ring_wait(0, 1)
    ring_start(0, 2)
    ring_start(1, 1)
    ring_wait(0, 2)
    ring_start(0, 3)
    dispatch(0, 0)
    ring_wait(1, 1)
    ring_start(1, 2)
    ring_wait(0, 3)
    ring_start(0, 4)
    ring_wait(1, 2)
    ring_start(1, 3)
    ring_wait(0, 4)
    dispatch(0, 1)
    dispatch(1, 0)
    ring_wait(1, 3)
    ring_start(1, 4)
    ring_wait(1, 4)
    dispatch(1, 1)

    for copy in own_copies:
        copy.wait()
    for copy in weight_copies:
        copy.wait_recv()

    ret = {}

    def send_back(t):
        for p in range(tiles):
            cols = pl.ds(p * TILE, TILE)
            for d in (2, 1, 3):
                copy = remote(results.at[t, :, :, d, :, cols], returned.at[t, x, :, :, :, cols],
                              ret_s.at[t, p, d], ret_r.at[t, p, d], at_x(NX - d))
                copy.start()
                ret[t, p, d] = copy
            copy = pltpu.make_async_copy(
                results.at[t, :, :, 0, :, cols], returned.at[t, x, :, :, :, cols], ret_s.at[t, p, 0])
            copy.start()
            ret[t, p, 0] = copy

    dispatched(0)

    def forward(j, carry):
        def project(n, carry):
            span = cols_of(n, 256)
            act[j, :, span] = dot_nt(arrived[0, j].reshape(rows, width), weights[j, span, :])
            return carry

        lax.fori_loop(0, 2 * full // 256, project, 0)
        gate = act[j, :, pl.ds(0, full)]
        sig = 1.0 / (1.0 + jnp.exp(-gate))
        hidden[j] = (gate * sig * act[j, :, pl.ds(full, full)]).astype(BF16)

        def down(n, carry):
            cols = cols_of(n)
            out = dot_nn(hidden[j], weights[j, pl.ds(2 * full, full), cols]).astype(BF16)
            results[0, j, :, :, :, cols] = out.reshape(2, NX, unit, TILE)
            return carry

        lax.fori_loop(0, tiles, down, 0)
        return carry

    lax.fori_loop(0, 2, forward, 0)
    send_back(0)

    dispatched(1)

    def backward(j, carry):
        back = dot_nt(arrived[1, j].reshape(rows, width), weights[j, pl.ds(2 * full, full), :])
        gate = act[j, :, pl.ds(0, full)]
        up = act[j, :, pl.ds(full, full)]
        sig = 1.0 / (1.0 + jnp.exp(-gate))
        grads[j, :, pl.ds(0, full)] = (back * up * sig * (1.0 + gate * (1.0 - sig))).astype(BF16)
        grads[j, :, pl.ds(full, full)] = (back * (gate * sig)).astype(BF16)

        def down(n, carry):
            cols = cols_of(n)
            out = dot_nn(grads[j], weights[j, pl.ds(0, 2 * full), cols]).astype(BF16)
            results[1, j, :, :, :, cols] = out.reshape(2, NX, unit, TILE)
            return carry

        lax.fori_loop(0, tiles, down, 0)
        return carry

    lax.fori_loop(0, 2, backward, 0)
    send_back(1)

    for copy in weight_copies:
        copy.wait_send()
    for t in range(2):
        for c in range(2):
            for d in range(1, NX):
                disp[t, c, d].wait_send()
    blocks = half // unit

    def weight_grads(j, carry):
        grads_t[...] = grads[j].T
        hidden_t[...] = hidden[j].T

        def tile(n, carry):
            cols = cols_of(n, 256)
            rows_in = arrived[0, j, :, :, :, cols].reshape(rows, 256)
            back_in = arrived[1, j, :, :, :, cols].reshape(rows, 256)
            for m in range(3):
                if m < 2:
                    total = dot_nn(grads_t[pl.ds(m * full, full), :], rows_in).astype(BF16)
                else:
                    total = dot_nn(hidden_t[...], back_in).astype(BF16)
                weights[j, pl.ds(m * full, half), cols] = total[:half]
                spot = pl.ds(m * 2 * blocks + j * blocks, blocks)
                sendrows[spot, :, cols] = total[half:].reshape(blocks, unit, 256)
            return carry

        lax.fori_loop(0, width // 256, tile, 0)
        return carry

    lax.fori_loop(0, 2, weight_grads, 0)
    wg_copies = []
    for m in range(3):
        spot = pl.ds(m * 2 * blocks, 2 * blocks)
        copy = remote(sendrows.at[spot], wrecv.at[spot], wg_s.at[m], wg_r.at[m], other_core)
        copy.start()
        wg_copies.append(copy)

    out_copies = []
    outs = (gate_out, up_out, down_out)

    def sum_replicas():
        for m in range(3):
            wg_copies[m].wait_recv()

            def tile(n, carry):
                cols = cols_of(n, 256)
                for j in range(2):
                    mine = weights[j, pl.ds(m * full, half), cols].astype(F32)
                    spot = pl.ds(m * 2 * blocks + j * blocks, blocks)
                    theirs = wrecv[spot, :, cols].reshape(half, 256).astype(F32)
                    weights[j, pl.ds(m * full, half), cols] = (mine + theirs).astype(BF16)
                return carry

            lax.fori_loop(0, width // 256, tile, 0)
            copy = pltpu.make_async_copy(
                weights.at[:, pl.ds(m * full, half)], outs[m], out_l.at[m])
            copy.start()
            out_copies.append(copy)

    for t in range(2):
        for way in range(2):
            for step in range(4):
                ring[t][way][step].wait_send()
    red = {}

    def reduce_copy(t, p, way, step):
        cols = pl.ds(p * TILE, TILE)
        if step == 1:
            spot, part = 1, pl.ds(way * half_rows, half_rows)
        else:
            spot, part = step + 3 * way, pl.ds(0, tokens)
        copy = remote(zrows.at[t, spot, part, cols], reduced.at[t, spot, part, cols],
                      red_s.at[t, p, way, step - 1], red_r.at[t, p, way, step - 1],
                      at_z(NZ - 1 if way == 0 else 1))
        red[t, p, way, step] = copy
        return copy

    def own_part(i, slot):
        return partial[i % 4, pl.ds(PLACE[slot] * tokens, tokens), :]

    def combine(i):
        t, p = divmod(i, tiles)
        cols = pl.ds(p * TILE, TILE)
        ret[t, p, 0].wait()
        for d in range(1, NX):
            ret[t, p, d].wait_recv()
        for c in range(2):
            back = returned[t, :, :, c, :, cols].reshape(rows, TILE)
            if t == 0:
                total = dot_nn(pick_hi[c], back) + dot_nn(pick_lo[c], back)
            else:
                total = dot_nn(pick_t[c], back)
            partial[i % 4, pl.ds(c * 4 * tokens, 4 * tokens), :] = total

    def reduce_step(i, step):
        t, p = divmod(i, tiles)
        cols = pl.ds(p * TILE, TILE)
        for way in range(2):
            slot = 5 - step if way == 0 else 3 + step
            mine = own_part(i, slot)
            if step == 1:
                part = pl.ds(way * half_rows, half_rows)
                zrows[t, 1, part, cols] = mine[way * half_rows:(way + 1) * half_rows].astype(BF16)
            else:
                red[t, p, way, step - 1].wait_recv()
                spot = step + 3 * way
                if step == 2:
                    part = pl.ds(way * half_rows, half_rows)
                    rest = pl.ds((1 - way) * half_rows, half_rows)
                    zrows[t, spot, part, cols] = (
                        mine[way * half_rows:(way + 1) * half_rows]
                        + reduced[t, 1, part, cols].astype(F32)).astype(BF16)
                    zrows[t, spot, rest, cols] = (
                        mine[(1 - way) * half_rows:(2 - way) * half_rows].astype(BF16))
                else:
                    zrows[t, spot, :, cols] = (
                        mine + reduced[t, spot - 1, :, cols].astype(F32)).astype(BF16)
            reduce_copy(t, p, way, step).start()

    hops = []

    def finish(i):
        t, p = divmod(i, tiles)
        cols = pl.ds(p * TILE, TILE)
        for way in range(2):
            red[t, p, way, 4].wait_recv()
        total = own_part(i, 0) + reduced[t, 4, :, cols].astype(F32) + reduced[t, 7, :, cols].astype(F32)
        final[t, :, cols] = (zrows[t, 0, :, cols].astype(F32) + total).astype(BF16)
        copy = remote(final.at[t, :, cols], (next_ref if t == 0 else prev_ref).at[:, cols],
                      hop_s.at[t, p], hop_r.at[t, p], sec_next if t == 0 else sec_prev)
        copy.start()
        hops.append(copy)

    items = 2 * tiles
    for i in range(items + 4):
        if i == 2:
            sum_replicas()
        if 0 <= i - 4:
            finish(i - 4)
        for step in (4, 3, 2):
            if 0 <= i - step + 1 < items:
                reduce_step(i - step + 1, step)
        if i < items:
            combine(i)
            reduce_step(i, 1)

    for copy in meta_copies:
        copy.wait_send()
    for copy in wg_copies:
        copy.wait_send()
    for t in range(2):
        for p in range(tiles):
            for d in range(1, NX):
                ret[t, p, d].wait_send()
    for copy in red.values():
        copy.wait_send()
    for copy in hops:
        copy.wait()
    for copy in out_copies:
        copy.wait()


def shards(
    row_codes, block_exponents, routes, route_weight, out_grad, gate_weight, up_weight, down_weight
):
    tokens, width = row_codes.shape[1:]
    local, half = gate_weight.shape[1:3]
    unit = 4 * CAP
    rows = NX * 2 * unit
    full = 2 * half
    tiles = width // TILE
    lanes = 4 * tokens
    routes_t = jnp.tile(routes[0].T, (1, 4))
    rweight_t = jnp.tile(route_weight[0].T, (1, 4))
    dma = pltpu.SemaphoreType.DMA
    any_spec = pl.BlockSpec(memory_space=pl.ANY)
    vmem_spec = pl.BlockSpec(memory_space=pltpu.VMEM)
    rows_type = jax.ShapeDtypeStruct((tokens, width), BF16)
    weight_type = jax.ShapeDtypeStruct((local, half, width), BF16)
    groups = NZ
    results = pl.pallas_call(
        kernel,
        out_shape=(rows_type, rows_type, weight_type, weight_type, weight_type),
        in_specs=[vmem_spec] * 5 + [any_spec] * 3,
        out_specs=[any_spec] * 5,
        scratch_shapes=[
            pltpu.VMEM((2, NZ, tokens, width), BF16),
            pltpu.VMEM((2 * 2 * NX * 2, unit, width), BF16),
            pltpu.VMEM((2, 2, 2, NX, unit, width), BF16),
            pltpu.VMEM((2, 3 * full, width), BF16),
            pltpu.VMEM((2, 2, 2, NX, unit, width), BF16),
            pltpu.VMEM((2, NX, 2, 2, unit, width), BF16),
            pltpu.VMEM((2, NZ, tokens, width), BF16),
            pltpu.VMEM((4, NZ * tokens, TILE), F32),
            pltpu.VMEM((3 * 2 * half // unit, unit, width), BF16),
            pltpu.VMEM((2, tokens, width), BF16),
            pltpu.VMEM((2, rows, 2 * full), F32),
            pltpu.VMEM((2, rows, full), BF16),
            pltpu.VMEM((full, rows), BF16),
            pltpu.VMEM((2, rows, 2 * full), BF16),
            pltpu.VMEM((2 * full, rows), BF16),
            pltpu.VMEM((groups, 2, 8, lanes), F32),
            pltpu.VMEM((groups, 2, 8, lanes), F32),
            pltpu.VMEM((2, rows, lanes), BF16),
            pltpu.VMEM((2, lanes, rows), BF16),
            pltpu.VMEM((2, lanes, rows), BF16),
            pltpu.VMEM((2, lanes, rows), BF16),
            pltpu.VMEM((2, rows, 128), F32),
            dma((2, 2, 4)), dma((2, 2, 4)),
            dma((NZ,)), dma((NZ,)),
            dma((3,)), dma((3,)), dma((3,)),
            dma((2, 2, NX)), dma((2, 2, NX)),
            dma((2, tiles, NX)), dma((2, tiles, NX)),
            dma((2, tiles, 2, 4)), dma((2, tiles, 2, 4)),
            dma((2, tiles)), dma((2, tiles)),
            dma((3,)), dma((3,)),
            dma((3,)),
        ],
        compiler_params=pltpu.CompilerParams(
            collective_id=0, has_side_effects=True, vmem_limit_bytes=62 * 2**20),
        cost_estimate=pl.CostEstimate(
            flops=12 * 10**9, bytes_accessed=16 * 10**6, transcendentals=10**6),
    )(
        row_codes[0], block_exponents[0], routes_t, rweight_t, out_grad[0],
        gate_weight[0], up_weight[0], down_weight[0],
    )
    return tuple(value[None] for value in results)


def solution(mesh):
    rows_spec = P("section", ("rep", "exp"), None)
    weight_spec = P("section", "exp", "rep", None)
    return jax.shard_map(
        shards,
        mesh=mesh,
        in_specs=(rows_spec,) * 5 + (weight_spec,) * 3,
        out_specs=(rows_spec,) * 2 + (weight_spec,) * 3,
        check_vma=False,
    )
```

profile of v0, /device:TPU:8, one launch (start us, length us, event | category | flops | bytes accessed | tf_op | source)
XLA Modules:
  0.0 203.5 jit_solution(11048641240294493603)
XLA Ops:
  0.6 0.7 tile.8
  1.3 0.7 tile.9.routes_ref
  2.0 0.7 tile.20
  2.7 0.7 tile.21.rweight_ref
  3.4 1.4 copy.13
  4.8 189.4 %shard_map.119 = (bf16[64,2048]{1,0:T(8,128)(2,1)}, bf16[64,2048]{1,0:T(8,128)(2,1)}, bf16[2,192,2048]{2,1,0:T(8,128)(2,1)}, bf16[2,192,2048]{2,1,0:T(8,128)(2,1)}, bf16[2,192,2048]{2,1,0:T(8,128)(2,1)}) custom-call(bf16[64,2048]{1,0:T(8,128)(2,1)} %bitcast.28, s32[64,16]{1,0:T(8,128)} %bitcast.22, s32[8,256]{1,0:T(8,128)} %tile.9.routes_ref, ...), custom_call_target="tpu_custom_call" | custom-call | flops 12000000000 | bytes 16000000 | tf_op jit(solution)/shard_map/pallas_call | solution.py:467
  194.2 1.7 copy.19
  195.9 1.7 copy.20
  197.6 0.0 copy-start.1
  197.6 2.8 %copy.21 = bf16[1,2,192,2048]{3,2,1,0:T(8,128)(2,1)} copy(bf16[1,2,192,2048]{3,2,1,0:T(8,128)(2,1)} %bitcast.19) | data formatting | bytes 3145728
  200.4 0.0 copy-done.1
  200.4 0.0 copy-start
  200.4 1.1 copy.22
  201.6 0.8 copy-done
  202.4 1.1 copy.23
Async XLA Ops:
  197.6 2.9 %copy-start.1 = (bf16[2,192,2048]{2,1,0:T(8,128)(2,1)S(1)}, bf16[2,192,2048]{2,1,0:T(8,128)(2,1)}, u32[]{:S(2)}) copy-start(bf16[2,192,2048]{2,1,0:T(8,128)(2,1)} %get-tuple-element.13) | copy-start | bytes 4718596
  200.4 2.0 copy-start
where the time goes:
time: 204 us
  Pallas kernels  189 us (93%)
  local copies, waits for them, and re-layouts  13.4 us (7%)
    pallas_call x1, Pallas kernels, shards(): pl.pallas_call(kernel, out_shape=(rows_type, rows_type, weight_type, weig...  189 us
    unnamed x10, local copies, waits for them, and re-layouts  10.7 us

commit v1 on v0

v1 whole, which is shorter than its diff:
```python
import functools

import jax
import jax.numpy as jnp
from jax import lax
from jax.experimental import pallas as pl
from jax.experimental.pallas import tpu as pltpu
from jax.sharding import PartitionSpec as P

MESH = pl.DeviceIdType.MESH
NX = 4
NZ = 8
CAP = 12
ORDER = (0, 1, 7, 2, 6, 3, 5, 4)
PLACE = tuple(ORDER.index(slot) for slot in range(NZ))
TILE = 512
BACK = tuple((0, start, TILE, False) for start in range(0, 2048, TILE)) + (
    (1, 0, 256, False), (1, 256, 512, False), (1, 768, 512, False), (1, 1280, 256, False),
    (1, 1536, 256, True), (1, 1792, 128, True), (1, 1920, 128, True))
AHEAD = 2
F32 = jnp.float32
BF16 = jnp.bfloat16


def dot_nn(a, b):
    return lax.dot_general(a, b, (((1,), (0,)), ((), ())), preferred_element_type=F32)


def dot_nt(a, b):
    return lax.dot_general(a, b, (((1,), (1,)), ((), ())), preferred_element_type=F32)


def kernel(
    codes_hbm, exps_hbm, routes_hbm, rweight_hbm, grad_hbm, gate_ref, up_ref, down_ref,
    next_ref, prev_ref, gate_out, up_out, down_out,
    codes_ref, exps_ref, routes_ref, rweight_ref, zrows, sendrows, arrived, weights, results, returned, reduced, partial, wrecv, final,
    act, hidden, hidden_t, grads, grads_t, meta_src, meta, pick, pick_t, pick_hi, pick_lo, slot_w,
    first_l, ring_s, ring_r, meta_s, meta_r, wt_l, wt_s, wt_r, disp_s, disp_r, ret_s, ret_r,
    red_s, red_r, hop_s, hop_r, wg_s, wg_r, out_l,
):
    tokens, width = codes_ref.shape
    unit = sendrows.shape[1]
    half_rows = tokens // 2
    rows = NX * 2 * unit
    half = gate_ref.shape[1]
    full = 2 * half
    tiles = width // TILE
    rep, sec, ex = lax.axis_index("rep"), lax.axis_index("section"), lax.axis_index("exp")
    sections = lax.axis_size("section")
    z, x = lax.div(ex, NX), lax.rem(ex, NX)

    def at_z(k):
        return (rep, sec, lax.rem(z + k, NZ) * NX + x)

    def at_x(k):
        return (rep, sec, z * NX + lax.rem(x + k, NX))

    other_core = (1 - rep, sec, ex)
    sec_next = (rep, lax.rem(sec + 1, sections), ex)
    sec_prev = (rep, lax.rem(sec + sections - 1, sections), ex)

    def remote(src, dst, send, recv, device):
        copy = pltpu.make_async_remote_copy(
            src_ref=src, dst_ref=dst, send_sem=send, recv_sem=recv,
            device_id=device, device_id_type=MESH)
        return copy

    def cols_of(n, size=TILE):
        return pl.ds(pl.multiple_of(n * size, size), size)

    first_copies = []
    for m, (src, dst) in enumerate((
            (exps_hbm, exps_ref), (codes_hbm, codes_ref), (routes_hbm, routes_ref),
            (rweight_hbm, rweight_ref), (grad_hbm, zrows.at[1, 0]))):
        copy = pltpu.make_async_copy(src, dst, first_l.at[m])
        copy.start()
        first_copies.append(copy)
    weight_refs = (gate_ref, up_ref, down_ref)
    own_copies = []
    for m in range(3):
        copy = pltpu.make_async_copy(
            weight_refs[m], weights.at[:, pl.ds(m * full, half)], wt_l.at[m])
        copy.start()
        own_copies.append(copy)
    partners = [at_z(k) for k in range(1, NZ)] + [at_x(k) for k in range(1, NX)]
    partners += [other_core, sec_next, sec_prev]
    barrier = pltpu.get_barrier_semaphore()
    for device in partners:
        pl.semaphore_signal(barrier, inc=1, device_id=device, device_id_type=MESH)

    first_copies[0].wait()
    first_copies[1].wait()
    scale = jnp.exp2(exps_ref[...].astype(F32)).astype(BF16)
    for p in range(tiles):
        cols = pl.ds(p * TILE, TILE)
        block = lax.broadcasted_iota(jnp.int32, (scale.shape[0], TILE), 1) + p * TILE
        chosen = jnp.where(
            lax.div(block, width // scale.shape[0])
            == lax.broadcasted_iota(jnp.int32, (scale.shape[0], TILE), 0), 1.0, 0.0).astype(BF16)
        wide = lax.dot_general(scale, chosen, (((0,), (0,)), ((), ())), preferred_element_type=F32)
        zrows[0, 0, :, cols] = (codes_ref[:, cols].astype(F32) * wide).astype(BF16)
    pl.semaphore_wait(barrier, len(partners))

    def ring_copy(i, way, step):
        t, p = divmod(i, tiles)
        cols = pl.ds(p * TILE, TILE)
        slot = step - 1 if way == 0 else (NZ - step + 1) % NZ
        there = step if way == 0 else NZ - step
        part = pl.ds(way * half_rows, half_rows) if step == NZ // 2 else pl.ds(0, tokens)
        return remote(zrows.at[t, PLACE[slot], part, cols], zrows.at[t, PLACE[there], part, cols],
                      ring_s.at[i, way, step - 1], ring_r.at[i, way, step - 1],
                      at_z(1 if way == 0 else NZ - 1))

    pieces = 2 * tiles
    ring = [[[ring_copy(i, way, step) for step in range(1, 5)] for way in range(2)] for i in range(pieces)]

    def ring_start(i, step):
        for way in range(2):
            if step > 1:
                ring[i][way][step - 2].wait_recv()
            ring[i][way][step - 1].start()

    ring_start(0, 1)
    ring_start(1, 1)
    first_copies[2].wait()
    first_copies[3].wait()
    experts = meta_src.shape[0] * 8
    lanes = 4 * tokens
    spread = jnp.where(
        lax.broadcasted_iota(jnp.int32, (tokens, lanes), 0)
        == lax.rem(lax.broadcasted_iota(jnp.int32, (tokens, lanes), 1), tokens), 1.0, 0.0).astype(BF16)
    routes_wide = dot_nn(routes_ref[...].astype(F32).astype(BF16), spread)
    rweight = rweight_ref[...]
    first = rweight.astype(BF16)
    rweight = rweight - first.astype(F32)
    second = rweight.astype(BF16)
    third = (rweight - second.astype(F32)).astype(BF16)
    rweight_wide = (dot_nn(first, spread) + dot_nn(second, spread)) + dot_nn(third, spread)
    expert_id = lax.broadcasted_iota(jnp.int32, (experts, lanes), 0).astype(F32)
    hit = jnp.zeros((experts, lanes), F32)
    weight = jnp.zeros((experts, lanes), F32)
    for k in range(routes_ref.shape[0]):
        same = routes_wide[k:k + 1, :] == expert_id
        hit = jnp.where(same, 1.0, hit)
        weight = jnp.where(same, rweight_wide[k:k + 1, :], weight)
    earlier = lax.broadcasted_iota(jnp.int32, (128, lanes), 0)
    later = lax.rem(lax.broadcasted_iota(jnp.int32, (128, lanes), 1), tokens)
    before = jnp.where((earlier < later) & (earlier < tokens), 1.0, 0.0).astype(BF16)
    count = dot_nn(hit[:, :128].astype(BF16), before)
    slots = jnp.where(hit > 0.5, count, -1.0)
    for g in range(NZ):
        meta_src[g, 0] = slots[g * 8:(g + 1) * 8]
        meta_src[g, 1] = weight[g * 8:(g + 1) * 8]

    meta_copies = []
    for k in range(1, NZ):
        copy = remote(meta_src.at[lax.rem(z + k, NZ)], meta.at[k], meta_s.at[k], meta_r.at[k], at_z(k))
        copy.start()
        meta_copies.append(copy)

    meta_own = pltpu.make_async_copy(meta_src.at[z], meta.at[0], meta_s.at[0])
    meta_own.start()

    weight_copies = []
    for m in range(3):
        copy = remote(weight_refs[m], weights.at[:, pl.ds(m * full + half, half)],
                      wt_s.at[m], wt_r.at[m], other_core)
        copy.start()
        weight_copies.append(copy)

    first_copies[4].wait()
    lane_of = lax.broadcasted_iota(jnp.int32, (unit, lanes), 1)
    row_of = lax.broadcasted_iota(jnp.int32, (unit, lanes), 0)
    target = jnp.where(lax.div(lane_of, tokens) == lax.div(row_of, CAP), lax.rem(row_of, CAP), -5).astype(F32)
    source_of = lax.div(lax.broadcasted_iota(jnp.int32, (8, lanes), 1), tokens)

    def gathered(c, which):
        found = jnp.zeros((8, lanes), F32)
        for q in range(4):
            found = jnp.where(source_of == q, meta[ORDER[4 * c + q], which], found)
        return found

    def make_pick(c):
        slot_cat = gathered(c, 0)
        for e in range(8):
            same = slot_cat[e:e + 1, :] == target
            pick[c, pl.ds(e * unit, unit), :] = jnp.where(same, 1.0, 0.0).astype(BF16)

    def make_weights(c):
        slot_cat, weight_cat = gathered(c, 0), gathered(c, 1)
        for e in range(8):
            same = slot_cat[e:e + 1, :] == target
            weighted = jnp.where(same, weight_cat[e:e + 1, :], 0.0)
            span = pl.ds(e * unit, unit)
            slot_w[c, span, :] = jnp.broadcast_to(jnp.sum(weighted, axis=1, keepdims=True), (unit, 128))
            act[c, span, pl.ds(0, lanes)] = weighted
            act[c, span, pl.ds(lanes, lanes)] = jnp.where(same, 1.0, 0.0)

    disp = {}

    def dispatch(i, c):
        t, p = divmod(i, tiles)
        cols = pl.ds(p * TILE, TILE)
        base = (t * 2 + c) * NX * 2
        taken = zrows[t, pl.ds(4 * c, 4), :, cols].reshape(4 * tokens, TILE)
        chosen = dot_nn(pick[c], taken)
        if t == 1:
            chosen = chosen * slot_w[c][:, :1]
        sendrows[pl.ds(base, 2 * NX), :, cols] = chosen.astype(BF16).reshape(2 * NX, unit, TILE)
        for d in (2, 1, 3):
            copy = remote(sendrows.at[pl.ds(base + 2 * lax.rem(x + d, NX), 2), :, cols],
                          arrived.at[t, :, c, d, :, cols],
                          disp_s.at[i, c, d], disp_r.at[i, c, d], at_x(d))
            copy.start()
            disp[i, c, d] = copy
        copy = pltpu.make_async_copy(
            sendrows.at[pl.ds(base + 2 * x, 2), :, cols], arrived.at[t, :, c, 0, :, cols],
            disp_s.at[i, c, 0])
        copy.start()
        disp[i, c, 0] = copy

    def dispatched(t):
        for i in range(t * tiles, (t + 1) * tiles):
            for c in range(2):
                disp[i, c, 0].wait()
                for d in range(1, NX):
                    disp[i, c, d].wait_recv()

    for turn in range(1, pieces + 4):
        for step in (4, 3, 2, 1):
            for i in range(pieces):
                if max(i, 1) - 2 + step == turn:
                    ring_start(i, step)
        if turn == 1:
            meta_own.wait()
            for copy in meta_copies:
                copy.wait_recv()
            make_pick(0)
        for i in range(pieces):
            if max(i, 1) + 3 == turn:
                for way in range(2):
                    ring[i][way][3].wait_recv()
                dispatch(i, 1)
        for i in range(pieces):
            if max(i, 1) + 1 == turn:
                dispatch(i, 0)
        if turn == 2:
            make_pick(1)
        if turn == 3:
            make_weights(0)
            make_weights(1)

    for c in range(2):
        weighted_t = act[c, :, pl.ds(0, lanes)].T
        high = weighted_t.astype(BF16)
        pick_hi[c] = high
        pick_lo[c] = (weighted_t - high.astype(F32)).astype(BF16)
        pick_t[c] = act[c, :, pl.ds(lanes, lanes)].T.astype(BF16)

    for copy in own_copies:
        copy.wait()
    for copy in weight_copies:
        copy.wait_recv()

    ret = {}

    def send_back(i):
        t, start, size, _ = BACK[i]
        cols = pl.ds(start, size)
        for d in (2, 1, 3):
            copy = remote(results.at[t, :, :, d, :, cols], returned.at[t, x, :, :, :, cols],
                          ret_s.at[i, d], ret_r.at[i, d], at_x(NX - d))
            copy.start()
            ret[i, d] = copy
        copy = pltpu.make_async_copy(
            results.at[t, :, :, 0, :, cols], returned.at[t, x, :, :, :, cols], ret_s.at[i, 0])
        copy.start()
        ret[i, 0] = copy

    dispatched(0)

    def forward(j, carry):
        def project(n, carry):
            span = cols_of(n, 256)
            act[j, :, span] = dot_nt(arrived[0, j].reshape(rows, width), weights[j, span, :])
            return carry

        lax.fori_loop(0, 2 * full // 256, project, 0)
        gate = act[j, :, pl.ds(0, full)]
        sig = 1.0 / (1.0 + jnp.exp(-gate))
        hidden[j] = (gate * sig * act[j, :, pl.ds(full, full)]).astype(BF16)

        def down(n, carry):
            cols = cols_of(n)
            out = dot_nn(hidden[j], weights[j, pl.ds(2 * full, full), cols]).astype(BF16)
            results[0, j, :, :, :, cols] = out.reshape(2, NX, unit, TILE)
            return carry

        lax.fori_loop(0, tiles, down, 0)
        return carry

    lax.fori_loop(0, 2, forward, 0)
    for i in range(tiles):
        send_back(i)

    dispatched(1)

    def backward(j, carry):
        back = dot_nt(arrived[1, j].reshape(rows, width), weights[j, pl.ds(2 * full, full), :])
        gate = act[j, :, pl.ds(0, full)]
        up = act[j, :, pl.ds(full, full)]
        sig = 1.0 / (1.0 + jnp.exp(-gate))
        grads[j, :, pl.ds(0, full)] = (back * up * sig * (1.0 + gate * (1.0 - sig))).astype(BF16)
        grads[j, :, pl.ds(full, full)] = (back * (gate * sig)).astype(BF16)

        def down(n, carry):
            cols = cols_of(n)
            out = dot_nn(grads[j], weights[j, pl.ds(0, 2 * full), cols]).astype(BF16)
            results[1, j, :, :, :, cols] = out.reshape(2, NX, unit, TILE)
            return carry

        lax.fori_loop(0, tiles, down, 0)
        return carry

    lax.fori_loop(0, 2, backward, 0)
    for i in range(tiles, tiles + AHEAD):
        send_back(i)

    for copy in weight_copies:
        copy.wait_send()
    for i in range(pieces):
        for c in range(2):
            for d in range(1, NX):
                disp[i, c, d].wait_send()
    blocks = half // unit

    def weight_grads(j, carry):
        grads_t[...] = grads[j].T
        hidden_t[...] = hidden[j].T

        def tile(n, carry):
            cols = cols_of(n, 256)
            rows_in = arrived[0, j, :, :, :, cols].reshape(rows, 256)
            back_in = arrived[1, j, :, :, :, cols].reshape(rows, 256)
            for m in range(3):
                if m < 2:
                    total = dot_nn(grads_t[pl.ds(m * full, full), :], rows_in).astype(BF16)
                else:
                    total = dot_nn(hidden_t[...], back_in).astype(BF16)
                weights[j, pl.ds(m * full, half), cols] = total[:half]
                spot = pl.ds(m * 2 * blocks + j * blocks, blocks)
                sendrows[spot, :, cols] = total[half:].reshape(blocks, unit, 256)
            return carry

        lax.fori_loop(0, width // 256, tile, 0)
        return carry

    lax.fori_loop(0, 2, weight_grads, 0)
    wg_copies = []
    for m in range(3):
        spot = pl.ds(m * 2 * blocks, 2 * blocks)
        copy = remote(sendrows.at[spot], wrecv.at[spot], wg_s.at[m], wg_r.at[m], other_core)
        copy.start()
        wg_copies.append(copy)

    out_copies = []
    outs = (gate_out, up_out, down_out)

    def sum_replicas():
        for m in range(3):
            wg_copies[m].wait_recv()

            def tile(n, carry):
                cols = cols_of(n, 256)
                for j in range(2):
                    mine = weights[j, pl.ds(m * full, half), cols].astype(F32)
                    spot = pl.ds(m * 2 * blocks + j * blocks, blocks)
                    theirs = wrecv[spot, :, cols].reshape(half, 256).astype(F32)
                    weights[j, pl.ds(m * full, half), cols] = (mine + theirs).astype(BF16)
                return carry

            lax.fori_loop(0, width // 256, tile, 0)
            copy = pltpu.make_async_copy(
                weights.at[:, pl.ds(m * full, half)], outs[m], out_l.at[m])
            copy.start()
            out_copies.append(copy)

    for i in range(pieces):
        for way in range(2):
            for step in range(4):
                ring[i][way][step].wait_send()
    red = {}

    def own_part(i, slot):
        return partial[i % 4, pl.ds(PLACE[slot] * tokens, tokens), pl.ds(0, BACK[i][2])]

    def combine(i):
        t, start, size, _ = BACK[i]
        cols = pl.ds(start, size)
        ret[i, 0].wait()
        for d in range(1, NX):
            ret[i, d].wait_recv()
        if tiles <= i < len(BACK) - AHEAD:
            send_back(i + AHEAD)
        for c in range(2):
            back = returned[t, :, :, c, :, cols].reshape(rows, size)
            if t == 0:
                total = dot_nn(pick_hi[c], back) + dot_nn(pick_lo[c], back)
            else:
                total = dot_nn(pick_t[c], back)
            partial[i % 4, pl.ds(c * 4 * tokens, 4 * tokens), pl.ds(0, size)] = total

    def reduce_start(i, spot, part, device, kind):
        t, start, size, _ = BACK[i]
        cols = pl.ds(start, size)
        copy = remote(zrows.at[t, spot[0], part, cols], reduced.at[t, spot[1], part, cols],
                      red_s.at[i, kind], red_r.at[i, kind], device)
        copy.start()
        red[i, kind] = copy

    def reduce_direct(i):
        t, start, size, _ = BACK[i]
        cols = pl.ds(start, size)
        for slot in (4, 3, 5, 2, 6, 1, 7):
            zrows[t, PLACE[slot], :, cols] = own_part(i, slot).astype(BF16)
            reduce_start(i, (PLACE[slot], slot), pl.ds(0, tokens), at_z(NZ - slot), slot)

    def reduce_step(i, step):
        t, start, size, _ = BACK[i]
        cols = pl.ds(start, size)
        for way in range(2):
            slot = 5 - step if way == 0 else 3 + step
            mine = own_part(i, slot)
            part, spot = pl.ds(0, tokens), step + 3 * way
            if step == 1:
                part, spot = pl.ds(way * half_rows, half_rows), 1
                zrows[t, 1, part, cols] = mine[way * half_rows:(way + 1) * half_rows].astype(BF16)
            else:
                red[i, way * 4 + step - 2].wait_recv()
                if step == 2:
                    got = pl.ds(way * half_rows, half_rows)
                    rest = pl.ds((1 - way) * half_rows, half_rows)
                    zrows[t, spot, got, cols] = (
                        mine[way * half_rows:(way + 1) * half_rows]
                        + reduced[t, 1, got, cols].astype(F32)).astype(BF16)
                    zrows[t, spot, rest, cols] = (
                        mine[(1 - way) * half_rows:(2 - way) * half_rows].astype(BF16))
                else:
                    zrows[t, spot, :, cols] = (
                        mine + reduced[t, spot - 1, :, cols].astype(F32)).astype(BF16)
            reduce_start(i, (spot, spot), part, at_z(NZ - 1 if way == 0 else 1), way * 4 + step - 1)

    hops = []

    def finish(i):
        t, start, size, direct = BACK[i]
        cols = pl.ds(start, size)
        total = own_part(i, 0)
        if direct:
            for slot in range(1, NZ):
                red[i, slot].wait_recv()
                total = total + reduced[t, slot, :, cols].astype(F32)
        else:
            for way in range(2):
                red[i, way * 4 + 3].wait_recv()
                total = total + reduced[t, 4 + 3 * way, :, cols].astype(F32)
        final[t, :, cols] = (zrows[t, 0, :, cols].astype(F32) + total).astype(BF16)
        copy = remote(final.at[t, :, cols], (next_ref if t == 0 else prev_ref).at[:, cols],
                      hop_s.at[i], hop_r.at[i], sec_next if t == 0 else sec_prev)
        copy.start()
        hops.append(copy)

    items = len(BACK)
    ended = 0
    for turn in range(items + 4):
        if turn == 2:
            sum_replicas()
        while ended < items and (turn >= ended + 4 or turn >= items and BACK[ended][3]):
            finish(ended)
            ended += 1
        for step in (4, 3, 2):
            i = turn - step + 1
            if 0 <= i < items and not BACK[i][3]:
                reduce_step(i, step)
        if turn < items:
            combine(turn)
            if BACK[turn][3]:
                reduce_direct(turn)
            else:
                reduce_step(turn, 1)

    for copy in meta_copies:
        copy.wait_send()
    for copy in wg_copies:
        copy.wait_send()
    for i in range(items):
        for d in range(1, NX):
            ret[i, d].wait_send()
    for copy in red.values():
        copy.wait_send()
    for copy in hops:
        copy.wait()
    for copy in out_copies:
        copy.wait()


def place_kernel(*refs):
    sems_in, sems_out = refs[-2:]
    held = refs[:-2]
    count = len(held) // 3
    inward, outward = [], []
    for m in range(count):
        source, target, middle = held[m], held[count + m], held[2 * count + m]
        parts = 2 if len(source.shape) == 3 else 1
        for h in range(parts):
            view = [ref.at[h] if parts == 2 else ref for ref in (source, target, middle)]
            inward.append(pltpu.make_async_copy(view[0], view[2], sems_in.at[m, h]))
            outward.append(pltpu.make_async_copy(view[2], view[1], sems_out.at[m, h]))
            inward[-1].start()
    for first, second in zip(inward, outward):
        first.wait()
        second.start()
    for copy in outward:
        copy.wait()


def shards(
    row_codes, block_exponents, routes, route_weight, out_grad, gate_weight, up_weight, down_weight
):
    tokens, width = row_codes.shape[1:]
    local, half = gate_weight.shape[1:3]
    unit = 4 * CAP
    rows = NX * 2 * unit
    full = 2 * half
    tiles = width // TILE
    lanes = 4 * tokens
    dma = pltpu.SemaphoreType.DMA
    any_spec = pl.BlockSpec(memory_space=pl.ANY)
    rows_type = jax.ShapeDtypeStruct((tokens, width), BF16)
    weight_type = jax.ShapeDtypeStruct((local, half, width), BF16)
    groups = NZ
    results = pl.pallas_call(
        kernel,
        out_shape=(rows_type, rows_type, weight_type, weight_type, weight_type),
        in_specs=[any_spec] * 8,
        out_specs=[any_spec] * 5,
        scratch_shapes=[
            pltpu.VMEM((tokens, width), BF16),
            pltpu.VMEM((block_exponents.shape[2], tokens), jnp.int32),
            pltpu.VMEM((routes.shape[2], tokens), jnp.int32),
            pltpu.VMEM((routes.shape[2], tokens), F32),
            pltpu.VMEM((2, NZ, tokens, width), BF16),
            pltpu.VMEM((2 * 2 * NX * 2, unit, width), BF16),
            pltpu.VMEM((2, 2, 2, NX, unit, width), BF16),
            pltpu.VMEM((2, 3 * full, width), BF16),
            pltpu.VMEM((2, 2, 2, NX, unit, width), BF16),
            pltpu.VMEM((2, NX, 2, 2, unit, width), BF16),
            pltpu.VMEM((2, NZ, tokens, width), BF16),
            pltpu.VMEM((4, NZ * tokens, TILE), F32),
            pltpu.VMEM((3 * 2 * half // unit, unit, width), BF16),
            pltpu.VMEM((2, tokens, width), BF16),
            pltpu.VMEM((2, rows, 2 * full), F32),
            pltpu.VMEM((2, rows, full), BF16),
            pltpu.VMEM((full, rows), BF16),
            pltpu.VMEM((2, rows, 2 * full), BF16),
            pltpu.VMEM((2 * full, rows), BF16),
            pltpu.VMEM((groups, 2, 8, lanes), F32),
            pltpu.VMEM((groups, 2, 8, lanes), F32),
            pltpu.VMEM((2, rows, lanes), BF16),
            pltpu.VMEM((2, lanes, rows), BF16),
            pltpu.VMEM((2, lanes, rows), BF16),
            pltpu.VMEM((2, lanes, rows), BF16),
            pltpu.VMEM((2, rows, 128), F32),
            dma((5,)),
            dma((2 * tiles, 2, 4)), dma((2 * tiles, 2, 4)),
            dma((NZ,)), dma((NZ,)),
            dma((3,)), dma((3,)), dma((3,)),
            dma((2 * tiles, 2, NX)), dma((2 * tiles, 2, NX)),
            dma((len(BACK), NX)), dma((len(BACK), NX)),
            dma((len(BACK), 8)), dma((len(BACK), 8)),
            dma((len(BACK),)), dma((len(BACK),)),
            dma((3,)), dma((3,)),
            dma((3,)),
        ],
        compiler_params=pltpu.CompilerParams(
            collective_id=0, has_side_effects=True, vmem_limit_bytes=62 * 2**20),
        cost_estimate=pl.CostEstimate(
            flops=12 * 10**9, bytes_accessed=16 * 10**6, transcendentals=10**6),
    )(
        row_codes[0], block_exponents[0].T, routes[0].T, route_weight[0].T, out_grad[0],
        gate_weight[0], up_weight[0], down_weight[0],
    )
    results = pl.pallas_call(
        place_kernel,
        out_shape=tuple(jax.ShapeDtypeStruct(value.shape, value.dtype) for value in results),
        in_specs=[any_spec] * 5,
        out_specs=[any_spec] * 5,
        scratch_shapes=[pltpu.VMEM(value.shape, value.dtype) for value in results] + [dma((5, 2)), dma((5, 2))],
        compiler_params=pltpu.CompilerParams(vmem_limit_bytes=62 * 2**20),
    )(*results)
    return tuple(value[None] for value in results)


def solution(mesh):
    rows_spec = P("section", ("rep", "exp"), None)
    weight_spec = P("section", "exp", "rep", None)
    return jax.shard_map(
        shards,
        mesh=mesh,
        in_specs=(rows_spec,) * 5 + (weight_spec,) * 3,
        out_specs=(rows_spec,) * 2 + (weight_spec,) * 3,
        check_vma=False,
    )
```

time: 204 us -> 186 us (0.912)
  local copies, waits for them, and re-layouts: 13.4 us -> 0 us
  Pallas kernels: 189 us -> 186 us
    unnamed x10 -> x0, local copies, waits for them, and re-layouts: 10.7 us -> none
    pallas_call x1, Pallas kernels: 189 us -> 181 us  [shards(): pl.pallas_call(kernel, out_shape=(rows_type, rows_type, weight_type, weig...]
    pallas_call x0 -> x1, Pallas kernels: none -> 4.84 us  [shards(): pl.pallas_call(place_kernel, out_shape=tuple((jax.ShapeDtypeStruct(value....]
    another operation x4 -> x0, local copies, waits for them, and re-layouts: 2.74 us -> none  [the longest x2 1.37 us: shards(): routes_t = jnp.tile(routes[0].T, (1, 4))]
where the time goes in v1:
time: 186 us
  Pallas kernels  186 us (100%)
    pallas_call x1, Pallas kernels, shards(): pl.pallas_call(kernel, out_shape=(rows_type, rows_type, weight_type, weig...  181 us
    pallas_call x1, Pallas kernels, shards(): pl.pallas_call(place_kernel, out_shape=tuple((jax.ShapeDtypeStruct(value....  4.84 us

profile of v1, /device:TPU:8, one launch (start us, length us, event | category | flops | bytes accessed | tf_op | source)
XLA Modules:
  0.0 186.3 jit_solution(12957430767665898563)
XLA Ops:
  0.6 180.7 %shard_map.119 = (bf16[64,2048]{1,0:T(8,128)(2,1)}, bf16[64,2048]{1,0:T(8,128)(2,1)}, bf16[2,192,2048]{2,1,0:T(8,128)(2,1)}, bf16[2,192,2048]{2,1,0:T(8,128)(2,1)}, bf16[2,192,2048]{2,1,0:T(8,128)(2,1)}) custom-call(bf16[64,2048]{1,0:T(8,128)(2,1)} %bitcast.25, s32[16,64]{1,0:T(8,128)} %bitcast.29, s32[8,64]{1,0:T(8,128)} %bitcast.30, f32[8,64]{1,0:T(8,128)} %bitcast.31, ...), custom_call_target="tpu_custom_call" | custom-call | flops 12000000000 | bytes 16000000 | tf_op jit(solution)/shard_map/pallas_call | solution.py:542
  181.3 4.8 %shard_map.120 = (bf16[64,2048]{1,0:T(8,128)(2,1)}, bf16[64,2048]{1,0:T(8,128)(2,1)}, bf16[2,192,2048]{2,1,0:T(8,128)(2,1)}, bf16[2,192,2048]{2,1,0:T(8,128)(2,1)}, bf16[2,192,2048]{2,1,0:T(8,128)(2,1)}) custom-call(bf16[64,2048]{1,0:T(8,128)(2,1)} %get-tuple-element.15.refs_0_, bf16[64,2048]{1,0:T(8,128)(2,1)} %get-tuple-element.16.refs_1_, ...), custom_call_target="tpu_custom_call" | custom-call | tf_op jit(solution)/shard_map/pallas_call | solution.py:593

commit v2 on v1

--- a/solution.py
+++ b/solution.py
@@ -16,7 +16,7 @@
 TILE = 512
 BACK = tuple((0, start, TILE, False) for start in range(0, 2048, TILE)) + (
     (1, 0, 256, False), (1, 256, 512, False), (1, 768, 512, False), (1, 1280, 256, False),
-    (1, 1536, 256, True), (1, 1792, 128, True), (1, 1920, 128, True))
+    (1, 1536, 256, False), (1, 1792, 256, True))
 AHEAD = 2
 F32 = jnp.float32
 BF16 = jnp.bfloat16
@@ -91,7 +91,8 @@
     first_copies[0].wait()
     first_copies[1].wait()
     scale = jnp.exp2(exps_ref[...].astype(F32)).astype(BF16)
-    for p in range(tiles):
+
+    def scale_rows(p):
         cols = pl.ds(p * TILE, TILE)
         block = lax.broadcasted_iota(jnp.int32, (scale.shape[0], TILE), 1) + p * TILE
         chosen = jnp.where(
@@ -99,6 +100,8 @@
             == lax.broadcasted_iota(jnp.int32, (scale.shape[0], TILE), 0), 1.0, 0.0).astype(BF16)
         wide = lax.dot_general(scale, chosen, (((0,), (0,)), ((), ())), preferred_element_type=F32)
         zrows[0, 0, :, cols] = (codes_ref[:, cols].astype(F32) * wide).astype(BF16)
+    scale_rows(0)
+    scale_rows(1)
     pl.semaphore_wait(barrier, len(partners))
 
     def ring_copy(i, way, step):
@@ -122,6 +125,8 @@
 
     ring_start(0, 1)
     ring_start(1, 1)
+    for p in range(2, tiles):
+        scale_rows(p)
     first_copies[2].wait()
     first_copies[3].wait()
     experts = meta_src.shape[0] * 8
@@ -231,6 +236,8 @@
             for i in range(pieces):
                 if max(i, 1) - 2 + step == turn:
                     ring_start(i, step)
+                    if step == 3:
+                        dispatch(i, 0)
         if turn == 1:
             meta_own.wait()
             for copy in meta_copies:
@@ -241,9 +248,6 @@
                 for way in range(2):
                     ring[i][way][3].wait_recv()
                 dispatch(i, 1)
-        for i in range(pieces):
-            if max(i, 1) + 1 == turn:
-                dispatch(i, 0)
         if turn == 2:
             make_pick(1)
         if turn == 3:
@@ -513,7 +517,10 @@
         source, target, middle = held[m], held[count + m], held[2 * count + m]
         parts = 2 if len(source.shape) == 3 else 1
         for h in range(parts):
-            view = [ref.at[h] if parts == 2 else ref for ref in (source, target, middle)]
+            if parts == 1:
+                view = (source, target, middle)
+            else:
+                view = [ref.at[h] for ref in (source, target, middle)]
             inward.append(pltpu.make_async_copy(view[0], view[2], sems_in.at[m, h]))
             outward.append(pltpu.make_async_copy(view[2], view[1], sems_out.at[m, h]))
             inward[-1].start()

time: 186 us -> 184 us (0.989)
  Pallas kernels: 186 us -> 183 us
    pallas_call x1, Pallas kernels: 181 us -> 178 us  [shards(): pl.pallas_call(kernel, out_shape=(rows_type, rows_type, weight_type, weig...]
where the time goes in v2:
time: 184 us
  Pallas kernels  183 us (99%)
    pallas_call x1, Pallas kernels, shards(): pl.pallas_call(kernel, out_shape=(rows_type, rows_type, weight_type, weig...  178 us
    pallas_call x1, Pallas kernels, shards(): pl.pallas_call(place_kernel, out_shape=tuple((jax.ShapeDtypeStruct(value....  4.84 us

profile of v2, /device:TPU:8, one launch (start us, length us, event | category | flops | bytes accessed | tf_op | source)
XLA Modules:
  0.0 183.7 jit_solution(2394834342625723654)
XLA Ops:
  0.6 178.1 %shard_map.119 = (bf16[64,2048]{1,0:T(8,128)(2,1)}, bf16[64,2048]{1,0:T(8,128)(2,1)}, bf16[2,192,2048]{2,1,0:T(8,128)(2,1)}, bf16[2,192,2048]{2,1,0:T(8,128)(2,1)}, bf16[2,192,2048]{2,1,0:T(8,128)(2,1)}) custom-call(bf16[64,2048]{1,0:T(8,128)(2,1)} %bitcast.25, s32[16,64]{1,0:T(8,128)} %bitcast.29, s32[8,64]{1,0:T(8,128)} %bitcast.30, f32[8,64]{1,0:T(8,128)} %bitcast.31, ...), custom_call_target="tpu_custom_call" | custom-call | flops 12000000000 | bytes 16000000 | tf_op jit(solution)/shard_map/pallas_call | solution.py:549
  178.7 4.8 %shard_map.120 = (bf16[64,2048]{1,0:T(8,128)(2,1)}, bf16[64,2048]{1,0:T(8,128)(2,1)}, bf16[2,192,2048]{2,1,0:T(8,128)(2,1)}, bf16[2,192,2048]{2,1,0:T(8,128)(2,1)}, bf16[2,192,2048]{2,1,0:T(8,128)(2,1)}) custom-call(bf16[64,2048]{1,0:T(8,128)(2,1)} %get-tuple-element.15.refs_0_, bf16[64,2048]{1,0:T(8,128)(2,1)} %get-tuple-element.16.refs_1_, ...), custom_call_target="tpu_custom_call" | custom-call | tf_op jit(solution)/shard_map/pallas_call | solution.py:600

commit v3 on v2

--- a/solution.py
+++ b/solution.py
@@ -17,7 +17,7 @@
 BACK = tuple((0, start, TILE, False) for start in range(0, 2048, TILE)) + (
     (1, 0, 256, False), (1, 256, 512, False), (1, 768, 512, False), (1, 1280, 256, False),
     (1, 1536, 256, False), (1, 1792, 256, True))
-AHEAD = 2
+AHEAD = 3
 F32 = jnp.float32
 BF16 = jnp.bfloat16
 

time: 184 us -> 184 us (level)
  no operation moved by 1% of the time
where the time goes in v3:
time: 184 us
  Pallas kernels  183 us (99%)
    pallas_call x1, Pallas kernels, shards(): pl.pallas_call(kernel, out_shape=(rows_type, rows_type, weight_type, weig...  178 us
    pallas_call x1, Pallas kernels, shards(): pl.pallas_call(place_kernel, out_shape=tuple((jax.ShapeDtypeStruct(value....  4.84 us

profile of v3, /device:TPU:8, one launch (start us, length us, event | category | flops | bytes accessed | tf_op | source)
XLA Modules:
  0.0 184.1 jit_solution(2260393035450827964)
XLA Ops:
  0.6 178.5 %shard_map.119 = (bf16[64,2048]{1,0:T(8,128)(2,1)}, bf16[64,2048]{1,0:T(8,128)(2,1)}, bf16[2,192,2048]{2,1,0:T(8,128)(2,1)}, bf16[2,192,2048]{2,1,0:T(8,128)(2,1)}, bf16[2,192,2048]{2,1,0:T(8,128)(2,1)}) custom-call(bf16[64,2048]{1,0:T(8,128)(2,1)} %bitcast.25, s32[16,64]{1,0:T(8,128)} %bitcast.29, s32[8,64]{1,0:T(8,128)} %bitcast.30, f32[8,64]{1,0:T(8,128)} %bitcast.31, ...), custom_call_target="tpu_custom_call" | custom-call | flops 12000000000 | bytes 16000000 | tf_op jit(solution)/shard_map/pallas_call | solution.py:549
  179.1 4.8 %shard_map.120 = (bf16[64,2048]{1,0:T(8,128)(2,1)}, bf16[64,2048]{1,0:T(8,128)(2,1)}, bf16[2,192,2048]{2,1,0:T(8,128)(2,1)}, bf16[2,192,2048]{2,1,0:T(8,128)(2,1)}, bf16[2,192,2048]{2,1,0:T(8,128)(2,1)}) custom-call(bf16[64,2048]{1,0:T(8,128)(2,1)} %get-tuple-element.15.refs_0_, bf16[64,2048]{1,0:T(8,128)(2,1)} %get-tuple-element.16.refs_1_, ...), custom_call_target="tpu_custom_call" | custom-call | tf_op jit(solution)/shard_map/pallas_call | solution.py:600
